TPU v7x, 32 devices: a whole 2x2x4 slice. The times are simulated.
32 devices in a mesh: row: 4 (over z), col: 2 (over x), clu: 4 (over y, core).
Axes of the slice: x: 2, y: 2, z: 4, core: 2. Of those that a mesh axis runs over, the one named last changes fastest.
Arguments:
- features: bfloat16 [1152, 1024], P(('row', 'col')), may hold values from 0 to 4, as said below
- weights_init: bfloat16 [1152, 1024], P(('row', 'col'), 'clu'), may hold values from 0.001 to 1
Outputs:
- log_assign: float32 [1152, 1024], P(('row', 'col'), 'clu')
Inputs may be any that keep to these rules, and one draw needn't show every extreme that they name: `features`: entries are zero or positive; every hit has at least 16 positive entries.
All inputs are finite; a program needn't handle non-finite values.
Results may differ from a plain program's by a relative error of at most 0.0076.
Values may be sent and summed in bfloat16 or wider, within the bound.
A program may use at most 64 MiB of HBM per device.

v0:
```python
import jax
import jax.numpy as jnp
from jax import lax
from jax.sharding import PartitionSpec as P

ITERS = 2


BETA = 320.0


def squared_norms(rows):
    widened = rows.astype(jnp.float32)
    return jnp.sum(widened * widened, axis=1)


def tanimoto(left, left_norms, right):
    gram = jnp.dot(left, right.T, preferred_element_type=jnp.float32)
    return (gram / (left_norms[:, None] + squared_norms(right)[None, :] - gram)).astype(
        jnp.bfloat16
    )


def on_device(features, weights_init):
    references = lax.all_gather(features, "row", axis=0, tiled=True)
    ref_norms = squared_norms(references)
    assign = weights_init
    log_assign = jnp.zeros(weights_init.shape, jnp.float32)
    for step in range(ITERS):
        moving = assign
        kernel_tile = tanimoto(
            references, ref_norms, lax.all_gather(features, "col", axis=0, tiled=True)
        )
        wide_partial = jnp.dot(
            kernel_tile,
            lax.all_gather(moving, "col", axis=0, tiled=True),
            preferred_element_type=jnp.float32,
        )
        products = lax.psum_scatter(wide_partial, "row", scatter_dimension=0, tiled=True)
        widened = assign.astype(jnp.float32)
        local_within = jnp.sum(widened * products, axis=0)
        size_sum, within = lax.psum((jnp.sum(widened, axis=0), local_within), ("row", "col"))
        size_sum = jnp.maximum(size_sum, 1.0)
        score = BETA * (
            2.0 * products / size_sum[None, :] - (within / (size_sum * size_sum))[None, :]
        )
        top = lax.pmax(jnp.max(score, axis=1), "clu")
        total = lax.psum(jnp.sum(jnp.exp(score - top[:, None]), axis=1), "clu")
        log_assign = score - top[:, None] - jnp.log(total)[:, None]
        assign = jnp.exp(log_assign).astype(jnp.bfloat16)
    return log_assign


def solution(mesh):
    placed = (P(("row", "col"), None), P(("row", "col"), "clu"))
    return jax.shard_map(
        on_device, mesh=mesh, in_specs=placed, out_specs=P(("row", "col"), "clu"), check_vma=False
    )
```

profile of v0, /device:TPU:0, one launch (start us, length us, event | category | flops | bytes accessed | tf_op | source)
XLA Modules:
  0.0 169.7 jit_solution(3786403846448441185)
XLA Ops:
  6.5 0.7 all-gather.2.cloned.1.call-update
  7.3 0.0 reduce-scatter.3.cloned.1.call-start
  7.3 6.2 %all_gather.15 = bf16[288,256]{1,0:T(8,128)(2,1)S(1)} all-gather(bf16[144,256]{1,0:T(8,128)(2,1)} %param.3), channel_id=1, replica_groups=mesh['row'=4,'col'=2,'clu'=4] {'col'}, dimensions={0}, use_global_device_ids=true | all-gather | bytes 221184 | tf_op jit(solution)/shard_map/all_gather | solution.py:36
  13.5 8.8 %all_gather.14 = bf16[288,1024]{1,0:T(8,128)(2,1)S(1)} all-gather(bf16[144,1024]{1,0:T(8,128)(2,1)} %param.2), channel_id=1, replica_groups=mesh['row'=4,'col'=2,'clu'=4] {'col'}, dimensions={0}, use_global_device_ids=true | all-gather | bytes 884736 | tf_op jit(solution)/shard_map/all_gather | solution.py:32
  22.3 0.2 multiply_reduce_fusion.1
  22.5 19.6 %all-gather.2.cloned.1.call-done = bf16[576,1024]{1,0:T(8,128)(2,1)} async-done(((bf16[144,1024]{1,0:T(8,128)(2,1)}), bf16[576,1024]{1,0:T(8,128)(2,1)}) %all-gather.2.cloned.1.call-update) | async-done | bytes 1179664 | tf_op jit(solution)/shard_map/all_gather | solution.py:25
  42.1 1.7 multiply_reduce_fusion
  43.8 0.0 copy-done.1
  43.8 0.7 fusion
  44.5 0.0 copy-start.2
  44.5 1.2 fusion.5
  45.6 0.0 reduce-scatter.3.cloned.1.call-update
  45.7 0.0 reduce-scatter.5.cloned.1.call-start
  45.7 21.2 %reduce-scatter.3.cloned.1.call-done = f32[144,256]{1,0:T(8,128)} async-done(((f32[576,256]{1,0:T(8,128)}), f32[144,256]{1,0:T(8,128)}) %reduce-scatter.3.cloned.1.call-update) | async-done | bytes 147472 | tf_op jit(solution)/shard_map/reduce_scatter | solution.py:39
  66.9 1.0 convert_reduce_fusion.1
  67.9 18.8 %all-reduce.1 = (f32[256]{0:T(256)S(1)}, f32[256]{0:T(256)S(1)}) all-reduce(f32[256]{0:T(256)S(1)} %get-tuple-element.8, f32[256]{0:T(256)S(1)} %get-tuple-element.7), channel_id=1, replica_groups=mesh['row'=4,'col'=2,'clu'=4] {'row','col'}, use_global_device_ids=true, to_apply=%region_6.0 | all-reduce | flops 512 | bytes 4096 | tf_op jit(solution)/shard_map/psum | solution.py:42
  86.7 1.0 fusion.4
  87.7 5.8 %pmax.14 = f32[144]{0:T(256)S(1)} all-reduce(f32[144]{0:T(256)S(1)} %fusion.4), channel_id=1, replica_groups=mesh['row'=4,'col'=2,'clu'=4] {'clu'}, use_global_device_ids=true, to_apply=%region_8.0 | all-reduce | flops 144 | bytes 1152 | tf_op jit(solution)/shard_map/pmax | solution.py:47
  93.5 1.1 exponential_reduce_fusion.1
  94.6 6.6 %psum.44 = f32[144]{0:T(256)S(1)} all-reduce(f32[144]{0:T(256)S(1)} %exponential_reduce_fusion.1), channel_id=1, replica_groups=mesh['row'=4,'col'=2,'clu'=4] {'clu'}, use_global_device_ids=true, to_apply=%region_10.0 | all-reduce | flops 144 | bytes 1152 | tf_op jit(solution)/shard_map/psum | solution.py:48
  101.2 1.0 exponential_convert_fusion
  102.3 5.0 %all_gather.16 = bf16[288,256]{1,0:T(8,128)(2,1)S(1)} all-gather(bf16[144,256]{1,0:T(8,128)(2,1)S(1)} %exponential_convert_fusion), channel_id=1, replica_groups=mesh['row'=4,'col'=2,'clu'=4] {'col'}, dimensions={0}, use_global_device_ids=true | all-gather | bytes 221184 | tf_op jit(solution)/shard_map/all_gather | solution.py:36
  107.3 1.2 fusion.6
  108.4 0.0 reduce-scatter.5.cloned.1.call-update
  108.5 18.8 %reduce-scatter.5.cloned.1.call-done = f32[144,256]{1,0:T(8,128)} async-done(((f32[576,256]{1,0:T(8,128)}), f32[144,256]{1,0:T(8,128)}) %reduce-scatter.5.cloned.1.call-update) | async-done | bytes 147472 | tf_op jit(solution)/shard_map/reduce_scatter | solution.py:39
  127.2 1.0 convert_reduce_fusion
  128.3 18.8 %all-reduce = (f32[256]{0:T(256)S(1)}, f32[256]{0:T(256)S(1)}) all-reduce(f32[256]{0:T(256)S(1)} %get-tuple-element.6, f32[256]{0:T(256)S(1)} %get-tuple-element.5), channel_id=1, replica_groups=mesh['row'=4,'col'=2,'clu'=4] {'row','col'}, use_global_device_ids=true, to_apply=%region_15.0 | all-reduce | flops 512 | bytes 4096 | tf_op jit(solution)/shard_map/psum | solution.py:42
  147.1 1.0 fusion.3
  148.1 5.7 %pmax.15 = f32[144]{0:T(256)S(1)} all-reduce(f32[144]{0:T(256)S(1)} %fusion.3), channel_id=1, replica_groups=mesh['row'=4,'col'=2,'clu'=4] {'clu'}, use_global_device_ids=true, to_apply=%region_17.0 | all-reduce | flops 144 | bytes 1152 | tf_op jit(solution)/shard_map/pmax | solution.py:47
  153.8 1.1 exponential_reduce_fusion
  154.9 6.6 %psum.47 = f32[144]{0:T(256)S(1)} all-reduce(f32[144]{0:T(256)S(1)} %exponential_reduce_fusion), channel_id=1, replica_groups=mesh['row'=4,'col'=2,'clu'=4] {'clu'}, use_global_device_ids=true, to_apply=%region_19.0 | all-reduce | flops 144 | bytes 1152 | tf_op jit(solution)/shard_map/psum | solution.py:48
  161.5 1.7 subtract_subtract_fusion
  (9 shorter events, 0.0 us)
Async XLA Ops:
  6.5 35.6 %all-gather.2.cloned.1.call-start = ((), (), s32[]{:S(2)}) async-start(), calls=%async_computation.2 | async-start | bytes 1474560 | tf_op jit(solution)/shard_map/all_gather | solution.py:25
  7.3 59.7 %reduce-scatter.3.cloned.1.call-start = ((), (), s32[]{:S(2)}) async-start(), calls=%async_computation.3 | async-start | bytes 737280 | tf_op jit(solution)/shard_map/reduce_scatter | solution.py:39
  42.1 1.7 copy-start.1
  44.5 22.4 %copy-start.2 = (bf16[144,256]{1,0:T(8,128)(2,1)S(1)}, bf16[144,256]{1,0:T(8,128)(2,1)}, u32[]{:S(2)}) copy-start(bf16[144,256]{1,0:T(8,128)(2,1)} %param.3) | copy-start | bytes 221188
  45.7 81.6 %reduce-scatter.5.cloned.1.call-start = ((), (), s32[]{:S(2)}) async-start(), calls=%async_computation.4 | async-start | bytes 737280 | tf_op jit(solution)/shard_map/reduce_scatter | solution.py:39
  87.7 39.5 %copy-start = (f32[144,256]{1,0:T(8,128)S(1)}, f32[144,256]{1,0:T(8,128)}, u32[]{:S(2)}) copy-start(f32[144,256]{1,0:T(8,128)} %reduce-scatter.3.cloned.1.call-done) | copy-start | bytes 442372
Sparse Core Ops, SparseCore 0:
  8.9 33.1 all-gather.1
  45.8 21.0 reduce-scatter.2
  108.6 18.5 reduce-scatter.4
where the time goes:
time: 170 us
  blocking collectives  82.2 us (48%)
  waiting for transfers between devices  60.3 us (35%)
  between operations  13.2 us (8%)
  other arithmetic  10.9 us (6%)
  matrix products  3 us (2%)
    reduce_scatter x2, waiting for transfers between devices, on_device(): lax.psum_scatter(wide_partial, 'row', scatter_dimension=0, tiled=True)  40 us
    psum x2, blocking collectives, on_device(): lax.psum((jnp.sum(widened, axis=0), local_within), ('row', 'col'))  37.6 us
    all_gather x1, waiting for transfers between devices, on_device(): references = lax.all_gather(features, 'row', axis=0, tiled=True)  19.6 us
    psum x2, blocking collectives, on_device(): total = lax.psum(jnp.sum(jnp.exp(score - top[:, None]), axis=1), 'clu')  13.2 us
    pmax x2, blocking collectives, on_device(): top = lax.pmax(jnp.max(score, axis=1), 'clu')  11.5 us
    all_gather x2, blocking collectives, on_device(): lax.all_gather(moving, 'col', axis=0, tiled=True)  11.2 us
    all_gather x1, blocking collectives, on_device(): lax.all_gather(features, 'col', axis=0, tiled=True)  8.75 us
  transfers between devices with their start and end apart: 3, of which 3 were waited for; matrix products, arithmetic and copies ran while one was open for 0% of the time, Pallas kernels for 0%

commit v1 on v0

--- a/solution.py
+++ b/solution.py
@@ -1,6 +1,10 @@
+import functools
+
 import jax
 import jax.numpy as jnp
 from jax import lax
+from jax.experimental import pallas as pl
+from jax.experimental.pallas import tpu as pltpu
 from jax.sharding import PartitionSpec as P
 
 ITERS = 2
@@ -51,8 +55,316 @@
     return log_assign
 
 
+def block_order(rows, cols):
+    near = [dz for dz in range(1, rows) if dz in (1, rows - 1)]
+    far = [dz for dz in range(1, rows) if dz not in near]
+    order = [(0, 0)] + [(0, dz) for dz in near]
+    order += [(dx, 0) for dx in range(1, cols)]
+    order += [(0, dz) for dz in far]
+    order += [(dx, dz) for dz in near + far for dx in range(1, cols)]
+    return order
+
+
+def strips_after(blocks, block, total):
+    done, plan = 0, {}
+    for n in range(1, blocks + 1):
+        ready = n * block
+        grain = 256 if n < blocks - 1 else 128
+        end = total if n == blocks else ready // grain * grain
+        if end > done:
+            plan[n] = (done, end)
+            done = end
+    return plan
+
+
+def tiles_of(lo, hi, size=256):
+    return [(a, min(a + size, hi)) for a in range(lo, hi, size)]
+
+
+def kernel(
+    rows,
+    cols,
+    feat,
+    weights,
+    out,
+    f_all,
+    w_all,
+    k_all,
+    a_all,
+    p_all,
+    norm_col,
+    norm_row,
+    stats,
+    stats_own,
+    local_sem,
+    f_send,
+    f_recv,
+    fx_send,
+    fz_send,
+    w_send,
+    wx_send,
+    w_recv,
+    s_send,
+    s_recv,
+):
+    block = feat.shape[0]
+    total, part = w_all.shape
+    quarter = f_all.shape[2]
+    blocks = rows * cols
+    z, x, q = lax.axis_index("row"), lax.axis_index("col"), lax.axis_index("clu")
+    y, c = q // 2, q % 2
+    order = block_order(rows, cols)
+    place = {b: i for i, b in enumerate(order)}
+
+    def row_peer(d):
+        return {"row": lax.rem(z + d, rows)}
+
+    def col_peer(d):
+        return {"col": lax.rem(x + d, cols)}
+
+    flip = [None, {"clu": y * 2 + 1 - c}, {"clu": (1 - y) * 2 + c}, {"clu": (1 - y) * 2 + 1 - c}]
+
+    def span(i):
+        return pl.ds(i * block, block)
+
+    def quarter_of(r):
+        index = q if r == 0 else flip[r]["clu"]
+        return feat.at[:, pl.ds(pl.multiple_of(index * quarter, quarter), quarter)]
+
+    own = []
+    for r in range(4):
+        own.append(
+            pltpu.make_async_copy(quarter_of(r), f_all.at[r, span(0)], local_sem.at[r])
+        )
+    own.append(pltpu.make_async_copy(weights, w_all.at[span(0)], local_sem.at[4]))
+    for copy in own:
+        copy.start()
+
+    barrier = pltpu.get_barrier_semaphore()
+    peers = [row_peer(d) for d in range(1, rows)] + [col_peer(d) for d in range(1, cols)] + flip[1:]
+    for peer in peers:
+        pl.semaphore_signal(barrier, inc=1, device_id=peer, device_id_type=pl.DeviceIdType.MESH)
+    pl.semaphore_wait(barrier, len(peers))
+
+    sent = []
+
+    def send(src, dst, send_sem, recv_sem, peer):
+        copy = pltpu.make_async_remote_copy(
+            src_ref=src,
+            dst_ref=dst,
+            send_sem=send_sem,
+            recv_sem=recv_sem,
+            device_id=peer,
+            device_id_type=pl.DeviceIdType.MESH,
+        )
+        copy.start()
+        sent.append(copy)
+
+    def arrived(dst, recv_sem):
+        pltpu.make_async_copy(dst, dst, recv_sem).wait()
+
+    def send_f_col(b, src):
+        for d in range(1, cols):
+            i = place[(cols - d, b[1])]
+            send(src, f_all.at[0, span(i)], fx_send.at[d, b[1]], f_recv.at[0, i], col_peer(d))
+
+    def send_w_col(b, src):
+        for d in range(1, cols):
+            i = place[(cols - d, b[1])]
+            send(src, w_all.at[span(i)], wx_send.at[d, b[1]], w_recv.at[i], col_peer(d))
+
+    send_f_col((0, 0), quarter_of(0))
+    for b in order[1:]:
+        if b[0] == 0:
+            i = place[(0, rows - b[1])]
+            send(quarter_of(0), f_all.at[0, span(i)], fz_send.at[b[1]], f_recv.at[0, i], row_peer(b[1]))
+    for b in order[1:]:
+        if b[0] == 0:
+            i = place[(0, rows - b[1])]
+            send(weights, w_all.at[span(i)], w_send.at[b[1]], w_recv.at[i], row_peer(b[1]))
+
+    for i, b in enumerate(order):
+        if i == 0:
+            continue
+        here = f_all.at[0, span(i)]
+        arrived(here, f_recv.at[0, i])
+        if b[0] == 0:
+            send_f_col(b, here)
+        send(here, f_all.at[2, span(i)], f_send.at[2, i], f_recv.at[2, i], flip[2])
+        send(here, f_all.at[1, span(i)], f_send.at[1, i], f_recv.at[1, i], flip[1])
+        if i == rows:
+            send_w_col((0, 0), weights)
+    for i, b in enumerate(order):
+        if i > 0 and b[0] == 0:
+            here = w_all.at[span(i)]
+            arrived(here, w_recv.at[i])
+            send_w_col(b, here)
+
+    def gram(a, b):
+        acc = None
+        for r in range(4):
+            g = lax.dot_general(
+                f_all[r, a[0] : a[1]],
+                f_all[r, b[0] : b[1]],
+                (((1,), (1,)), ((), ())),
+                preferred_element_type=jnp.float32,
+            )
+            acc = g if acc is None else acc + g
+        return acc
+
+    def ratio(g, a, b):
+        under = norm_col[a[0] : a[1], :] + norm_row[:, b[0] : b[1]] - g
+        return (g / under).astype(jnp.bfloat16)
+
+    def strip(lo, hi):
+        for t in tiles_of(lo, hi):
+            g = gram(t, t)
+            eye = lax.broadcasted_iota(jnp.int32, g.shape, 0) == lax.broadcasted_iota(
+                jnp.int32, g.shape, 1
+            )
+            diag = jnp.where(eye, g, 0.0)
+            norm_col[t[0] : t[1], :] = jnp.sum(diag, axis=1, keepdims=True)
+            norm_row[:, t[0] : t[1]] = jnp.sum(diag, axis=0, keepdims=True)
+            k_all[t[0] : t[1], t[0] : t[1]] = ratio(g, t, t)
+            for u in tiles_of(0, t[0]):
+                k_all[u[0] : u[1], t[0] : t[1]] = ratio(gram(u, t), u, t)
+                k_all[t[0] : t[1], u[0] : u[1]] = ratio(gram(t, u), t, u)
+
+    plan = strips_after(blocks, block, total)
+    for copy in own[:4]:
+        copy.wait()
+
+    def finish(i):
+        for r in (1, 3):
+            if i > 0:
+                arrived(f_all.at[r, span(i)], f_recv.at[r, i])
+        if i + 1 in plan:
+            strip(*plan[i + 1])
+
+    for i in range(1, blocks):
+        here = f_all.at[2, span(i)]
+        arrived(here, f_recv.at[2, i])
+        send(here, f_all.at[3, span(i)], f_send.at[3, i], f_recv.at[3, i], flip[1])
+        finish(i - 1)
+    finish(blocks - 1)
+
+    own[4].wait()
+    for i, b in enumerate(order):
+        if b[0] > 0:
+            arrived(w_all.at[span(i)], w_recv.at[i])
+    for t in tiles_of(0, total, 128):
+        a_all[:, t[0] : t[1]] = w_all[t[0] : t[1], :].astype(jnp.float32).T.astype(jnp.bfloat16)
+
+    wide = tiles_of(0, total, 384)
+    for step in range(ITERS):
+        last = step == ITERS - 1
+        size = jnp.zeros((part, 1), jnp.float32)
+        within = jnp.zeros((part, 1), jnp.float32)
+        for t in wide:
+            p = jnp.dot(a_all[...], k_all[:, t[0] : t[1]], preferred_element_type=jnp.float32)
+            p_all[:, t[0] : t[1]] = p
+            a = a_all[:, t[0] : t[1]].astype(jnp.float32)
+            size += jnp.sum(a, axis=1, keepdims=True)
+            within += jnp.sum(a * p, axis=1, keepdims=True)
+        size = jnp.maximum(size, 1.0)
+        scale = (2.0 * BETA) / size
+        shift = BETA * (within / (size * size))
+        span_all = [(0, -(-block // 128) * 128)] if last else wide
+        end = span_all[-1][1]
+        for t in span_all:
+            score = p_all[:, t[0] : t[1]] * scale - shift
+            p_all[:, t[0] : t[1]] = score
+            top = jnp.max(score, axis=0, keepdims=True)
+            stats_own[step, 0:1, t[0] : t[1]] = top
+            stats_own[step, 1:2, t[0] : t[1]] = jnp.sum(jnp.exp(score - top), axis=0, keepdims=True)
+        mine = stats_own.at[step, :, pl.ds(0, end)]
+        for r in (2, 3, 1):
+            send(
+                mine,
+                stats.at[step, r - 1, :, pl.ds(0, end)],
+                s_send.at[step, r - 1],
+                s_recv.at[step, r - 1],
+                flip[r],
+            )
+        for r in (1, 2, 3):
+            arrived(stats.at[step, r - 1, :, pl.ds(0, end)], s_recv.at[step, r - 1])
+        for t in span_all:
+            cut = slice(t[0], t[1])
+            tops = [stats_own[step, 0:1, cut]] + [stats[step, r, 0:1, cut] for r in range(3)]
+            sums = [stats_own[step, 1:2, cut]] + [stats[step, r, 1:2, cut] for r in range(3)]
+            top = functools.reduce(jnp.maximum, tops)
+            sum_all = sum(s * jnp.exp(m - top) for m, s in zip(tops, sums))
+            log_assign = p_all[:, cut] - top - jnp.log(sum_all)
+            if last:
+                out[...] = log_assign.T[:block, :]
+            else:
+                a_all[:, cut] = jnp.exp(log_assign).astype(jnp.bfloat16)
+
+    for copy in sent:
+        copy.wait_send()
+
+
+def fused(rows, cols, features, weights_init):
+    block, bits = features.shape
+    part = weights_init.shape[1]
+    blocks = rows * cols
+    total = block * blocks
+    dma = pltpu.SemaphoreType.DMA
+    flops = 2 * total * total * (bits + ITERS * part)
+    return pl.pallas_call(
+        functools.partial(kernel, rows, cols),
+        out_shape=jax.ShapeDtypeStruct((block, part), jnp.float32),
+        in_specs=[pl.BlockSpec(memory_space=pl.ANY)] * 2,
+        out_specs=pl.BlockSpec(memory_space=pltpu.VMEM),
+        scratch_shapes=[
+            pltpu.VMEM((4, total, bits // 4), jnp.bfloat16),
+            pltpu.VMEM((total, part), jnp.bfloat16),
+            pltpu.VMEM((total, total), jnp.bfloat16),
+            pltpu.VMEM((part, total), jnp.bfloat16),
+            pltpu.VMEM((part, total), jnp.float32),
+            pltpu.VMEM((total, 1), jnp.float32),
+            pltpu.VMEM((1, total), jnp.float32),
+            pltpu.VMEM((ITERS, 3, 2, total), jnp.float32),
+            pltpu.VMEM((ITERS, 2, total), jnp.float32),
+            dma((5,)),
+            dma((4, blocks)),
+            dma((4, blocks)),
+            dma((cols, rows)),
+            dma((rows,)),
+            dma((rows,)),
+            dma((cols, rows)),
+            dma((blocks,)),
+            dma((ITERS, 3)),
+            dma((ITERS, 3)),
+        ],
+        compiler_params=pltpu.CompilerParams(
+            collective_id=0, has_side_effects=True, vmem_limit_bytes=48 * 1024 * 1024
+        ),
+        cost_estimate=pl.CostEstimate(
+            flops=flops, bytes_accessed=4 * block * (bits + part), transcendentals=total * part
+        ),
+    )(features, weights_init)
+
+
+def fits(rows, cols, clus, hits, bits, clusters):
+    blocks = rows * cols
+    if clus != 4 or hits % blocks or hits % 128 or bits % 512 or clusters % 512:
+        return False
+    block = hits // blocks
+    held = 2 * hits * (bits + hits) + 10 * hits * (clusters // clus)
+    return block % 16 == 0 and rows > 1 and cols > 1 and held <= 16 * 1024 * 1024
+
+
 def solution(mesh):
     placed = (P(("row", "col"), None), P(("row", "col"), "clu"))
-    return jax.shard_map(
-        on_device, mesh=mesh, in_specs=placed, out_specs=P(("row", "col"), "clu"), check_vma=False
-    )
+    rows, cols, clus = (mesh.shape[a] for a in ("row", "col", "clu"))
+
+    def whole(features, weights_init):
+        hits, bits = features.shape
+        ok = fits(rows, cols, clus, hits, bits, weights_init.shape[1])
+        body = functools.partial(fused, rows, cols) if ok else on_device
+        return jax.shard_map(
+            body, mesh=mesh, in_specs=placed, out_specs=P(("row", "col"), "clu"), check_vma=False
+        )(features, weights_init)
+
+    return whole

time: 170 us -> 39.8 us (0.23)
  blocking collectives: 82.2 us -> 0 us
  waiting for transfers between devices: 60.3 us -> 0 us
  Pallas kernels: 0 us -> 37.1 us
  between operations: 13.2 us -> 0.01 us
  other arithmetic: 10.9 us -> 0 us
  matrix products: 3 us -> 0 us
  local copies, waits for them, and re-layouts: 0.03 us -> 2.51 us
    psum x4 -> x0, blocking collectives: 50.8 us -> none  [the longest x2 37.6 us: on_device(): lax.psum((jnp.sum(widened, axis=0), local_within), ('row', 'col'))]
    reduce_scatter x2 -> x0, waiting for transfers between devices: 40 us -> none  [on_device(): lax.psum_scatter(wide_partial, 'row', scatter_dimension=0, tiled=True)]
    pallas_call x0 -> x1, Pallas kernels: none -> 37.1 us  [fused(): pl.pallas_call(functools.partial(kernel, rows, cols), out_shape=jax.Shape...]
    all_gather x3 -> x0, blocking collectives: 20 us -> none  [the longest x2 11.2 us: on_device(): lax.all_gather(moving, 'col', axis=0, tiled=True)]
    all_gather x1 -> x0, waiting for transfers between devices: 19.6 us -> none  [on_device(): references = lax.all_gather(features, 'row', axis=0, tiled=True)]
    pmax x2 -> x0, blocking collectives: 11.5 us -> none  [on_device(): top = lax.pmax(jnp.max(score, axis=1), 'clu')]
    reduce_sum x6 -> x0, other arithmetic: 6.1 us -> none  [the longest x2 2.22 us: on_device(): total = lax.psum(jnp.sum(jnp.exp(score - top[:, None]), axis=1), 'clu')]
    dot_general x3 -> x0, matrix products: 3 us -> none  [the longest x2 2.32 us: on_device(): jnp.dot(kernel_tile, lax.all_gather(moving, 'col', axis=0, tiled=True), p...]
  transfers between devices with their start and end apart: 3 -> 0, of which waited for: 3 -> 0; matrix products, arithmetic and copies ran while one was open for 0% -> 0% of each run, Pallas kernels for 0% -> 0%
where the time goes in v1:
time: 39.8 us; the launch traced here: 39.6 us
  Pallas kernels  37.1 us (93%)
  local copies, waits for them, and re-layouts  2.51 us (6%)
    pallas_call x1, Pallas kernels, fused(): pl.pallas_call(functools.partial(kernel, rows, cols), out_shape=jax.Shape...  37.1 us
    unnamed x5, local copies, waits for them, and re-layouts  2.51 us

profile of v1, /device:TPU:0, one launch (start us, length us, event | category | flops | bytes accessed | tf_op | source)
XLA Modules:
  0.0 39.6 jit_solution(5062852693975515295)
XLA Ops:
  0.0 0.0 copy-start
  0.0 1.0 %copy-done = bf16[144,1024]{1,0:T(8,128)(2,1)S(1)} copy-done((bf16[144,1024]{1,0:T(8,128)(2,1)S(1)}, bf16[144,1024]{1,0:T(8,128)(2,1)}, u32[]{:S(2)}) %copy-start) | copy-done | bytes 294936
  1.0 0.0 copy-start.1
  1.0 0.9 %copy-done.1 = bf16[144,256]{1,0:T(8,128)(2,1)S(1)} copy-done((bf16[144,256]{1,0:T(8,128)(2,1)S(1)}, bf16[144,256]{1,0:T(8,128)(2,1)}, u32[]{:S(2)}) %copy-start.1) | copy-done | bytes 73752
  1.8 37.1 %shard_map.28 = f32[144,256]{1,0:T(8,128)S(1)} custom-call(bf16[144,1024]{1,0:T(8,128)(2,1)S(1)} %copy-done, bf16[144,256]{1,0:T(8,128)(2,1)S(1)} %copy-done.1), custom_call_target="tpu_custom_call" | custom-call | flops 4076863488 | bytes 737280 | tf_op jit(solution)/shard_map/pallas_call | solution.py:314
  39.0 0.7 %copy.4 = f32[144,256]{1,0:T(8,128)} copy(f32[144,256]{1,0:T(8,128)S(1)} %shard_map.28) | data formatting | bytes 294912
Async XLA Ops:
  0.0 1.0 %copy-start = (bf16[144,1024]{1,0:T(8,128)(2,1)S(1)}, bf16[144,1024]{1,0:T(8,128)(2,1)}, u32[]{:S(2)}) copy-start(bf16[144,1024]{1,0:T(8,128)(2,1)} %feat.1) | copy-start | bytes 884740
  1.0 0.9 %copy-start.1 = (bf16[144,256]{1,0:T(8,128)(2,1)S(1)}, bf16[144,256]{1,0:T(8,128)(2,1)}, u32[]{:S(2)}) copy-start(bf16[144,256]{1,0:T(8,128)(2,1)} %weights.1) | copy-start | bytes 221188

commit v2 on v1

--- a/solution.py
+++ b/solution.py
@@ -178,27 +178,34 @@
         if b[0] == 0:
             i = place[(0, rows - b[1])]
             send(quarter_of(0), f_all.at[0, span(i)], fz_send.at[b[1]], f_recv.at[0, i], row_peer(b[1]))
-    for b in order[1:]:
-        if b[0] == 0:
-            i = place[(0, rows - b[1])]
-            send(weights, w_all.at[span(i)], w_send.at[b[1]], w_recv.at[i], row_peer(b[1]))
+
+    def send_w_row(near):
+        for dz in range(1, rows):
+            if (dz in (1, rows - 1)) == near:
+                j = place[(0, rows - dz)]
+                send(weights, w_all.at[span(j)], w_send.at[dz], w_recv.at[j], row_peer(dz))
 
     for i, b in enumerate(order):
+        here = f_all.at[0, span(i)]
+        if i > 0:
+            arrived(here, f_recv.at[0, i])
+            if b[0] == 0:
+                send_f_col(b, here)
+            send(here, f_all.at[2, span(i)], f_send.at[2, i], f_recv.at[2, i], flip[2])
+            send(here, f_all.at[1, span(i)], f_send.at[1, i], f_recv.at[1, i], flip[1])
+        if i == 1:
+            send_w_row(True)
+        if i == 2:
+            send_w_row(False)
         if i == 0:
-            continue
-        here = f_all.at[0, span(i)]
-        arrived(here, f_recv.at[0, i])
-        if b[0] == 0:
-            send_f_col(b, here)
-        send(here, f_all.at[2, span(i)], f_send.at[2, i], f_recv.at[2, i], flip[2])
-        send(here, f_all.at[1, span(i)], f_send.at[1, i], f_recv.at[1, i], flip[1])
-        if i == rows:
             send_w_col((0, 0), weights)
-    for i, b in enumerate(order):
-        if i > 0 and b[0] == 0:
-            here = w_all.at[span(i)]
-            arrived(here, w_recv.at[i])
-            send_w_col(b, here)
+
+    def pass_weights():
+        for i, b in enumerate(order):
+            if i > 0 and b[0] == 0:
+                here = w_all.at[span(i)]
+                arrived(here, w_recv.at[i])
+                send_w_col(b, here)
 
     def gram(a, b):
         acc = None
@@ -246,6 +253,8 @@
         arrived(here, f_recv.at[2, i])
         send(here, f_all.at[3, span(i)], f_send.at[3, i], f_recv.at[3, i], flip[1])
         finish(i - 1)
+        if i == min(3, blocks - 1):
+            pass_weights()
     finish(blocks - 1)
 
     own[4].wait()

time: 39.8 us -> 38.4 us (0.965)
  Pallas kernels: 37.1 us -> 35.7 us
    pallas_call x1, Pallas kernels: 37.1 us -> 35.7 us  [fused(): pl.pallas_call(functools.partial(kernel, rows, cols), out_shape=jax.Shape...]
where the time goes in v2:
time: 38.4 us; the launch traced here: 38.3 us
  Pallas kernels  35.7 us (93%)
  local copies, waits for them, and re-layouts  2.51 us (7%)
    pallas_call x1, Pallas kernels, fused(): pl.pallas_call(functools.partial(kernel, rows, cols), out_shape=jax.Shape...  35.7 us
    unnamed x5, local copies, waits for them, and re-layouts  2.51 us

profile of v2, /device:TPU:0, one launch (start us, length us, event | category | flops | bytes accessed | tf_op | source)
XLA Modules:
  0.0 38.3 jit_solution(7324791117899605731)
XLA Ops:
  0.0 0.0 copy-start
  0.0 1.0 %copy-done = bf16[144,1024]{1,0:T(8,128)(2,1)S(1)} copy-done((bf16[144,1024]{1,0:T(8,128)(2,1)S(1)}, bf16[144,1024]{1,0:T(8,128)(2,1)}, u32[]{:S(2)}) %copy-start) | copy-done | bytes 294936
  1.0 0.0 copy-start.1
  1.0 0.9 %copy-done.1 = bf16[144,256]{1,0:T(8,128)(2,1)S(1)} copy-done((bf16[144,256]{1,0:T(8,128)(2,1)S(1)}, bf16[144,256]{1,0:T(8,128)(2,1)}, u32[]{:S(2)}) %copy-start.1) | copy-done | bytes 73752
  1.8 35.7 %shard_map.28 = f32[144,256]{1,0:T(8,128)S(1)} custom-call(bf16[144,1024]{1,0:T(8,128)(2,1)S(1)} %copy-done, bf16[144,256]{1,0:T(8,128)(2,1)S(1)} %copy-done.1), custom_call_target="tpu_custom_call" | custom-call | flops 4076863488 | bytes 737280 | tf_op jit(solution)/shard_map/pallas_call | solution.py:323
  37.6 0.7 %copy.4 = f32[144,256]{1,0:T(8,128)} copy(f32[144,256]{1,0:T(8,128)S(1)} %shard_map.28) | data formatting | bytes 294912
Async XLA Ops:
  0.0 1.0 %copy-start = (bf16[144,1024]{1,0:T(8,128)(2,1)S(1)}, bf16[144,1024]{1,0:T(8,128)(2,1)}, u32[]{:S(2)}) copy-start(bf16[144,1024]{1,0:T(8,128)(2,1)} %feat.1) | copy-start | bytes 884740
  1.0 0.9 %copy-start.1 = (bf16[144,256]{1,0:T(8,128)(2,1)S(1)}, bf16[144,256]{1,0:T(8,128)(2,1)}, u32[]{:S(2)}) copy-start(bf16[144,256]{1,0:T(8,128)(2,1)} %weights.1) | copy-start | bytes 221188

commit v3 on v2

--- a/solution.py
+++ b/solution.py
@@ -279,25 +279,25 @@
         scale = (2.0 * BETA) / size
         shift = BETA * (within / (size * size))
         span_all = [(0, -(-block // 128) * 128)] if last else wide
-        end = span_all[-1][1]
-        for t in span_all:
+        for n, t in enumerate(span_all):
             score = p_all[:, t[0] : t[1]] * scale - shift
             p_all[:, t[0] : t[1]] = score
             top = jnp.max(score, axis=0, keepdims=True)
             stats_own[step, 0:1, t[0] : t[1]] = top
             stats_own[step, 1:2, t[0] : t[1]] = jnp.sum(jnp.exp(score - top), axis=0, keepdims=True)
-        mine = stats_own.at[step, :, pl.ds(0, end)]
-        for r in (2, 3, 1):
-            send(
-                mine,
-                stats.at[step, r - 1, :, pl.ds(0, end)],
-                s_send.at[step, r - 1],
-                s_recv.at[step, r - 1],
-                flip[r],
-            )
-        for r in (1, 2, 3):
-            arrived(stats.at[step, r - 1, :, pl.ds(0, end)], s_recv.at[step, r - 1])
-        for t in span_all:
+            cells = pl.ds(t[0], t[1] - t[0])
+            for r in (2, 3, 1):
+                send(
+                    stats_own.at[step, :, cells],
+                    stats.at[step, r - 1, :, cells],
+                    s_send.at[step, n, r - 1],
+                    s_recv.at[step, n, r - 1],
+                    flip[r],
+                )
+        for n, t in enumerate(span_all):
+            cells = pl.ds(t[0], t[1] - t[0])
+            for r in (1, 2, 3):
+                arrived(stats.at[step, r - 1, :, cells], s_recv.at[step, n, r - 1])
             cut = slice(t[0], t[1])
             tops = [stats_own[step, 0:1, cut]] + [stats[step, r, 0:1, cut] for r in range(3)]
             sums = [stats_own[step, 1:2, cut]] + [stats[step, r, 1:2, cut] for r in range(3)]
@@ -343,8 +343,8 @@
             dma((rows,)),
             dma((cols, rows)),
             dma((blocks,)),
-            dma((ITERS, 3)),
-            dma((ITERS, 3)),
+            dma((ITERS, len(tiles_of(0, total, 384)), 3)),
+            dma((ITERS, len(tiles_of(0, total, 384)), 3)),
         ],
         compiler_params=pltpu.CompilerParams(
             collective_id=0, has_side_effects=True, vmem_limit_bytes=48 * 1024 * 1024

time: 38.4 us -> 38.6 us (level)
  no operation moved by 1% of the time
where the time goes in v3:
time: 38.6 us; the launch traced here: 38.4 us
  Pallas kernels  35.9 us (93%)
  local copies, waits for them, and re-layouts  2.51 us (7%)
    pallas_call x1, Pallas kernels, fused(): pl.pallas_call(functools.partial(kernel, rows, cols), out_shape=jax.Shape...  35.9 us
    unnamed x5, local copies, waits for them, and re-layouts  2.51 us

profile of v3, /device:TPU:0, one launch (start us, length us, event | category | flops | bytes accessed | tf_op | source)
XLA Modules:
  0.0 38.4 jit_solution(7779984944440259538)
XLA Ops:
  0.0 0.0 copy-start
  0.0 1.0 %copy-done = bf16[144,1024]{1,0:T(8,128)(2,1)S(1)} copy-done((bf16[144,1024]{1,0:T(8,128)(2,1)S(1)}, bf16[144,1024]{1,0:T(8,128)(2,1)}, u32[]{:S(2)}) %copy-start) | copy-done | bytes 294936
  1.0 0.0 copy-start.1
  1.0 0.9 %copy-done.1 = bf16[144,256]{1,0:T(8,128)(2,1)S(1)} copy-done((bf16[144,256]{1,0:T(8,128)(2,1)S(1)}, bf16[144,256]{1,0:T(8,128)(2,1)}, u32[]{:S(2)}) %copy-start.1) | copy-done | bytes 73752
  1.8 35.9 %shard_map.28 = f32[144,256]{1,0:T(8,128)S(1)} custom-call(bf16[144,1024]{1,0:T(8,128)(2,1)S(1)} %copy-done, bf16[144,256]{1,0:T(8,128)(2,1)S(1)} %copy-done.1), custom_call_target="tpu_custom_call" | custom-call | flops 4076863488 | bytes 737280 | tf_op jit(solution)/shard_map/pallas_call | solution.py:323
  37.7 0.7 %copy.4 = f32[144,256]{1,0:T(8,128)} copy(f32[144,256]{1,0:T(8,128)S(1)} %shard_map.28) | data formatting | bytes 294912
Async XLA Ops:
  0.0 1.0 %copy-start = (bf16[144,1024]{1,0:T(8,128)(2,1)S(1)}, bf16[144,1024]{1,0:T(8,128)(2,1)}, u32[]{:S(2)}) copy-start(bf16[144,1024]{1,0:T(8,128)(2,1)} %feat.1) | copy-start | bytes 884740
  1.0 0.9 %copy-start.1 = (bf16[144,256]{1,0:T(8,128)(2,1)S(1)}, bf16[144,256]{1,0:T(8,128)(2,1)}, u32[]{:S(2)}) copy-start(bf16[144,256]{1,0:T(8,128)(2,1)} %weights.1) | copy-start | bytes 221188
